TPU v7x, 768 devices: a whole 4x8x12 slice. The times are simulated.
768 devices in a mesh: dp: 96 (over z, y_hi, x), fsdp: 8 (over y_lo, core).
Axes of the slice: x: 4, y: 8 (y_hi: 2, y_lo: 4; y = y_hi * 4 + y_lo), z: 12, core: 2. Of those that a mesh axis runs over, the one named last changes fastest.
Arguments:
- hidden_in: bfloat16 [24576, 8192], P('dp', 'fsdp'), may hold values from -6 to 6
- grad_out: bfloat16 [24576, 24576], P('dp', 'fsdp'), may hold values from -0.0234375 to 0.0234375
- basis: bfloat16 [8192, 512], P('fsdp'), may hold values from -0.25 to 0.25
- first_moment: float32 [24576, 512], P(('fsdp', 'dp')), may hold values from -1.5 to 1.5
- second_moment: float32 [24576, 512], P(('fsdp', 'dp')), may hold values from 0.0001 to 0.01
Outputs:
- new_first: float32 [24576, 512], P(('fsdp', 'dp'))
- new_second: float32 [24576, 512], P(('fsdp', 'dp'))
- update: bfloat16 [8, 3072, 8192], P(None, 'dp', 'fsdp')
All inputs are finite; a program needn't handle non-finite values.
Results may differ from a plain program's by a relative error of at most 0.0058.
Values may be sent and summed in bfloat16 or wider, within the bound.
No kernel may reach another device: no remote copies, remote signals or barrier semaphores. Data moves between devices by JAX's collectives and lax.ppermute only.
A program may use at most 64 MiB of HBM per device.

v0:
```python
import jax
import jax.numpy as jnp
from jax import lax
from jax.sharding import PartitionSpec as P

STEP = 10


def shards(hidden_in, grad_out, basis, first_moment, second_moment):
    partial_reduced = jnp.dot(hidden_in, basis, preferred_element_type=jnp.float32)
    reduced = lax.psum(partial_reduced, "fsdp").astype(jnp.bfloat16)
    projected = lax.psum_scatter(
        lax.dot_general(
            grad_out, reduced, (((0,), (0,)), ((), ())), preferred_element_type=jnp.float32
        ),
        "dp",
        scatter_dimension=0,
        tiled=True,
    )
    new_first = 0.9 * first_moment + 0.1 * projected
    new_second = 0.999 * second_moment + 0.001 * projected * projected
    first_hat = new_first / (1.0 - 0.9**STEP)
    second_hat = new_second / (1.0 - 0.999**STEP)
    direction = (first_hat / (jnp.sqrt(second_hat) + 1e-08)).astype(jnp.bfloat16)
    grouped = lax.all_gather(direction[None], "fsdp", axis=0, tiled=True)
    update = jnp.einsum("grk,dk->grd", grouped, basis, preferred_element_type=jnp.float32)
    return (new_first, new_second, update.astype(jnp.bfloat16))


def solution(mesh):
    in_specs = (
        P("dp", "fsdp"),
        P("dp", "fsdp"),
        P("fsdp", None),
        P(("fsdp", "dp"), None),
        P(("fsdp", "dp"), None),
    )
    out_specs = (P(("fsdp", "dp"), None), P(("fsdp", "dp"), None), P(None, "dp", "fsdp"))
    return jax.shard_map(shards, mesh=mesh, in_specs=in_specs, out_specs=out_specs, check_vma=False)
```

profile of v0, /device:TPU:1, one launch (start us, length us, event | category | flops | bytes accessed | tf_op | source)
XLA Modules:
  0.0 759.9 jit_solution(1925269464488471661)
XLA Ops:
  7.2 0.0 copy-start
  7.2 0.0 reduce-scatter.4.cloned.1.call-start
  7.2 1.9 fusion.4
  9.2 39.3 %all-reduce.1 = bf16[256,512]{1,0:T(8,128)(2,1)S(1)} all-reduce(f32[256,512]{1,0:T(8,128)S(1)} %fusion.4), channel_id=1, replica_groups=mesh['dp'=96,'fsdp'=8] {'fsdp'}, use_global_device_ids=true, to_apply=%region_0.0 | all-reduce | flops 131072 | bytes 786432 | tf_op jit(solution)/shard_map/psum | solution.py:11
  48.5 0.0 copy-done
  48.5 3.7 convolution_bitcast_fusion
  52.2 6.6 copy.26
  58.8 0.0 copy-start.2
  58.8 0.0 copy-start.3
  58.8 0.0 copy-start.1
  58.8 0.0 reduce-scatter.4.cloned.1.call-update
  58.8 597.6 %reduce-scatter.4.cloned.1.call-done = f32[32,512]{1,0:T(8,128)} async-done(((f32[3072,512]{1,0:T(8,128)}), f32[32,512]{1,0:T(8,128)}) %reduce-scatter.4.cloned.1.call-update) | async-done | bytes 65552 | tf_op jit(solution)/shard_map/reduce_scatter | solution.py:12
  656.4 0.0 copy-done.2
  656.4 0.0 copy-done.3
  656.4 1.5 divide_convert_fusion
  658.0 93.8 %all-gather = bf16[256,512]{1,0:T(8,128)(2,1)S(1)} all-gather(bf16[32,512]{1,0:T(8,128)(2,1)S(1)} %get-tuple-element.12), channel_id=2, replica_groups=mesh['dp'=96,'fsdp'=8] {'fsdp'}, dimensions={0}, use_global_device_ids=true | all-gather | bytes 294912 | tf_op jit(solution)/shard_map/all_gather | solution.py:25
  751.8 0.0 copy-done.1
  751.8 1.3 convolution_convert_fusion
Async XLA Ops:
  7.2 41.3 %copy-start = (bf16[256,3072]{1,0:T(8,128)(2,1)S(1)}, bf16[256,3072]{1,0:T(8,128)(2,1)}, u32[]{:S(2)}) copy-start(bf16[256,3072]{1,0:T(8,128)(2,1)} %param.6) | copy-start | bytes 4718596
  7.2 649.2 %reduce-scatter.4.cloned.1.call-start = ((), (), s32[]{:S(2)}) async-start(), calls=%async_computation.1 | async-start | bytes 6356992 | tf_op jit(solution)/shard_map/reduce_scatter | solution.py:12
  58.8 597.7 %copy-start.2 = (f32[32,512]{1,0:T(8,128)S(1)}, f32[32,512]{1,0:T(8,128)}, u32[]{:S(2)}) copy-start(f32[32,512]{1,0:T(8,128)} %param.9) | copy-start | bytes 196612
  58.8 597.7 %copy-start.3 = (f32[32,512]{1,0:T(8,128)S(1)}, f32[32,512]{1,0:T(8,128)}, u32[]{:S(2)}) copy-start(f32[32,512]{1,0:T(8,128)} %param.8) | copy-start | bytes 196612
  58.8 693.0 %copy-start.1 = (bf16[1024,512]{1,0:T(8,128)(2,1)S(1)}, bf16[1024,512]{1,0:T(8,128)(2,1)}, u32[]{:S(2)}) copy-start(bf16[1024,512]{1,0:T(8,128)(2,1)} %param.7) | copy-start | bytes 3145732
Sparse Core Ops, SparseCore 0:
  58.9 597.4 reduce-scatter.3
where the time goes:
time: 760 us
  waiting for transfers between devices  598 us (79%)
  blocking collectives  133 us (18%)
  between operations  14.1 us (2%)
    reduce_scatter x1, waiting for transfers between devices, shards(): lax.psum_scatter(lax.dot_general(grad_out, reduced, (((0,), (0,)), ((), (...  598 us
    all_gather x1, blocking collectives, shards(): grouped = lax.all_gather(direction[None], 'fsdp', axis=0, tiled=True)  93.8 us
    psum x1, blocking collectives, shards(): reduced = lax.psum(partial_reduced, 'fsdp').astype(jnp.bfloat16)  39.3 us
  transfers between devices with their start and end apart: 1, of which 1 were waited for; matrix products, arithmetic and copies ran while one was open for 0% of the time, Pallas kernels for 0%

commit v1 on v0

v1 whole, which is shorter than its diff:
```python
import jax
import jax.numpy as jnp
from jax import lax
from jax.experimental import pallas as pl
from jax.experimental.pallas import tpu as pltpu
from jax.sharding import Mesh, PartitionSpec as P

STEP = 10
AXES = ("z", "h", "x", "y", "c")
SIZES = (12, 2, 4, 4, 2)
SWAP = ((0, 1), (1, 0))


def project(grad_ref, mine_ref, other_ref, out_ref):
    first = lax.axis_index("c") == 0
    total = None
    for x in range(grad_ref.shape[0]):
        mine, other = mine_ref[x], other_ref[x]
        low = jnp.where(first, mine, other)
        high = jnp.where(first, other, mine)
        reduced = jnp.concatenate([low, high], axis=0)
        term = jnp.dot(grad_ref[x], reduced, preferred_element_type=jnp.float32)
        total = term if total is None else total + term
    out_ref[...] = total.astype(out_ref.dtype)


def shards(hidden_in, grad_out, basis, first_moment, second_moment):
    f32, bf16 = jnp.float32, jnp.bfloat16
    rows = first_moment.shape[0]
    rank = basis.shape[1]
    tokens = hidden_in.shape[0]
    piece = tokens // 8
    turned = grad_out.T.reshape(24, 4, rows, tokens).transpose(1, 0, 2, 3).reshape(4, 24 * rows, tokens)

    partial = jnp.dot(hidden_in, basis, preferred_element_type=f32).astype(bf16)
    partial, turned = lax.optimization_barrier((partial, turned))
    spread = lax.all_to_all(turned, "x", 0, 0, tiled=True)
    partial = lax.all_to_all(partial, ("c", "y"), 0, 0, tiled=True).reshape(8, piece, rank)
    reduced = jnp.sum(partial.astype(f32), axis=0).astype(bf16)
    copies = jnp.broadcast_to(reduced[None], (16, piece, rank)).reshape(-1, rank)
    mine = lax.all_to_all(copies, ("x", "y"), 0, 0, tiled=True).reshape(4, 4 * piece, rank)
    other = lax.ppermute(mine, "c", SWAP)

    part = pl.pallas_call(
        project,
        out_shape=jax.ShapeDtypeStruct((24 * rows, rank), bf16),
        in_specs=[pl.BlockSpec(memory_space=pltpu.VMEM)] * 3,
        out_specs=pl.BlockSpec(memory_space=pltpu.VMEM),
        compiler_params=pltpu.CompilerParams(vmem_limit_bytes=32 * 1024 * 1024),
        cost_estimate=pl.CostEstimate(flops=2 * 24 * rows * 4 * tokens * rank, bytes_accessed=4 << 20, transcendentals=0),
    )(spread, mine, other)
    part = lax.all_to_all(part, ("z", "h"), 0, 0, tiled=True).reshape(24, rows, rank)
    projected = jnp.sum(part.astype(f32), axis=0)

    new_first = 0.9 * first_moment + 0.1 * projected
    new_second = 0.999 * second_moment + 0.001 * projected * projected
    first_hat = new_first / (1.0 - 0.9**STEP)
    second_hat = new_second / (1.0 - 0.999**STEP)
    direction = (first_hat / (jnp.sqrt(second_hat) + 1e-08)).astype(bf16)
    copies = jnp.broadcast_to(direction[None], (8, rows, rank)).reshape(-1, rank)
    grouped = lax.all_to_all(copies, ("y", "c"), 0, 0, tiled=True)
    update = lax.dot_general(grouped, basis, (((1,), (1,)), ((), ())), preferred_element_type=f32)
    return (new_first, new_second, update.astype(bf16).reshape(8, rows, -1))


def solution(mesh):
    fine = Mesh(mesh.devices.reshape(SIZES), AXES)
    dp, fsdp = ("z", "h", "x"), ("y", "c")
    in_specs = (P(dp, fsdp), P(dp, fsdp), P(fsdp, None), P(fsdp + dp, None), P(fsdp + dp, None))
    out_specs = (P(fsdp + dp, None), P(fsdp + dp, None), P(None, dp, fsdp))
    return jax.shard_map(shards, mesh=fine, in_specs=in_specs, out_specs=out_specs, check_vma=False)
```

time: 760 us -> 132 us (0.17)
  waiting for transfers between devices: 598 us -> 15.9 us
  blocking collectives: 133 us -> 100 us
  between operations: 14.1 us -> 0.74 us
    reduce_scatter x1 -> x0, waiting for transfers between devices: 598 us -> none  [shards(): lax.psum_scatter(lax.dot_general(grad_out, reduced, (((0,), (0,)), ((), (...]
    all_to_all x0 -> x4, blocking collectives: none -> 100 us  [the longest x1 41.6 us: shards(): lax.all_to_all(part, ('z', 'h'), 0, 0, tiled=True).reshape(24, rows, rank)]
    all_gather x1 -> x0, blocking collectives: 93.8 us -> none  [shards(): grouped = lax.all_gather(direction[None], 'fsdp', axis=0, tiled=True)]
    psum x1 -> x0, blocking collectives: 39.3 us -> none  [shards(): reduced = lax.psum(partial_reduced, 'fsdp').astype(jnp.bfloat16)]
    all_to_all x0 -> x1, waiting for transfers between devices: none -> 15.9 us  [shards(): spread = lax.all_to_all(turned, 'x', 0, 0, tiled=True)]
  transfers between devices with their start and end apart: 1 -> 2, of which waited for: 1 -> 1; matrix products, arithmetic and copies ran while one was open for 0% -> 0% of each run, Pallas kernels for 0% -> 0%
where the time goes in v1:
time: 132 us
  blocking collectives  100 us (76%)
  waiting for transfers between devices  15.9 us (12%)
  starting transfers between devices  6.93 us (5%)
  local copies, waits for them, and re-layouts  3.21 us (2%)
  Pallas kernels  2.02 us (2%)
  matrix products  1.71 us (1%)
    all_to_all x1, blocking collectives, shards(): lax.all_to_all(part, ('z', 'h'), 0, 0, tiled=True).reshape(24, rows, rank)  41.6 us
    all_to_all x1, blocking collectives, shards(): lax.all_to_all(partial, ('c', 'y'), 0, 0, tiled=True)  22 us
    all_to_all x1, blocking collectives, shards(): lax.all_to_all(copies, ('x', 'y'), 0, 0, tiled=True)  18.6 us
    all_to_all x1, blocking collectives, shards(): grouped = lax.all_to_all(copies, ('y', 'c'), 0, 0, tiled=True)  18.2 us
    all_to_all x1, waiting for transfers between devices, shards(): spread = lax.all_to_all(turned, 'x', 0, 0, tiled=True)  15.9 us
    all_to_all x1, starting transfers between devices, shards(): spread = lax.all_to_all(turned, 'x', 0, 0, tiled=True)  3.56 us
    ppermute x1, starting transfers between devices, shards(): other = lax.ppermute(mine, 'c', SWAP)  3.37 us
  transfers between devices with their start and end apart: 2, of which 1 were waited for; matrix products, arithmetic and copies ran while one was open for 0% of the time, Pallas kernels for 0%

profile of v1, /device:TPU:1, one launch (start us, length us, event | category | flops | bytes accessed | tf_op | source)
XLA Modules:
  0.0 131.7 jit_solution(12959800430380921423)
XLA Ops:
  0.6 0.0 copy-start
  0.6 1.8 %copy.9 = bf16[256,3072]{0,1:T(8,128)(2,1)S(1)} copy(bf16[256,3072]{1,0:T(8,128)(2,1)} %param.6) | data formatting | bytes 3145728 | tf_op args[1]
  2.4 0.0 copy-start.1
  2.5 1.3 %copy.10 = bf16[4,24,32,256]{3,2,1,0:T(8,128)(2,1)} copy(bf16[4,24,32,256]{3,2,0,1:T(8,128)(2,1)S(1)} %bitcast.19) | data formatting | bytes 3145728 | tf_op jit(solution)/shard_map/transpose | solution.py:33
  3.8 0.0 copy-done
  3.8 0.0 copy-done.1
  3.8 0.4 convolution_convert_fusion.1
  4.2 22.0 %all_to_all.38 = bf16[8,32,512]{2,1,0:T(8,128)(2,1)S(1)} all-to-all(bf16[8,32,512]{2,1,0:T(8,128)(2,1)S(1)} %bitcast.21), channel_id=1, replica_groups=mesh['z'=12,'h'=2,'x'=4,'y'=4,'c'=2] {'c','y'}, dimensions={0} | all-to-all | bytes 524288 | tf_op jit(solution)/shard_map/all_to_all | solution.py:38
  26.3 18.6 %all_to_all.39 = bf16[16,32,512]{2,1,0:T(8,128)(2,1)S(1)} all-to-all(bf16[16,32,512]{2,1,0:T(8,128)(2,1)S(1)} %broadcast_in_dim.4), channel_id=1, replica_groups=mesh['z'=12,'h'=2,'x'=4,'y'=4,'c'=2] {'x','y'}, dimensions={0} | all-to-all | bytes 1048576 | tf_op jit(solution)/shard_map/all_to_all | solution.py:41
  44.9 3.6 %all-to-all-start = ((bf16[4,768,256]{2,1,0:T(8,128)(2,1)}), bf16[4,768,256]{2,1,0:T(8,128)(2,1)S(1)}, u32[]{:S(2)}, u32[]{:S(2)}) async-start(bf16[4,768,256]{2,1,0:T(8,128)(2,1)} %bitcast.18), calls=%async_computation | async-start | bytes 3145728 | tf_op jit(solution)/shard_map/all_to_all | solution.py:37
  48.5 3.4 %collective-permute-start = (bf16[4,128,512]{2,1,0:T(8,128)(2,1)S(1)}, bf16[4,128,512]{2,1,0:T(8,128)(2,1)}, u32[]{:S(2)}, u32[]{:S(2)}) collective-permute-start(bf16[4,128,512]{2,1,0:T(8,128)(2,1)S(1)} %bitcast.16), channel_id=1, source_target_pairs={{0,1},{1,0},{2,3},{3,2},{4,5},{5,4},{6,7},{7,6},{8,9},{9,8},{10,11... | collective-permute-start | bytes 1572872 | tf_op jit(solution)/shard_map/ppermute | solution.py:42
  51.9 15.9 %all-to-all-done.grad_ref = bf16[4,768,256]{2,1,0:T(8,128)(2,1)S(1)} async-done(((bf16[4,768,256]{2,1,0:T(8,128)(2,1)}), bf16[4,768,256]{2,1,0:T(8,128)(2,1)S(1)}, u32[]{:S(2)}, u32[]{:S(2)}) %all-to-all-start) | async-done | bytes 1572896 | tf_op jit(solution)/shard_map/all_to_all | solution.py:37
  67.8 0.0 collective-permute-done.other_ref
  67.8 2.0 %shard_map.76 = bf16[768,512]{1,0:T(8,128)(2,1)S(1)} custom-call(bf16[4,768,256]{2,1,0:T(8,128)(2,1)S(1)} %all-to-all-done.grad_ref, bf16[4,128,512]{2,1,0:T(8,128)(2,1)S(1)} %bitcast.17, bf16[4,128,512]{2,1,0:T(8,128)(2,1)} %collective-permute-done.other_ref), custom_call_target="tpu_custom_call" | custom-call | flops 805306368 | bytes 4194304 | tf_op jit(solution)/shard_map/pallas_call | solution.py:44
  69.8 0.0 copy-start.2
  69.8 0.0 copy-start.3
  69.8 41.6 %all_to_all.40 = bf16[24,32,512]{2,1,0:T(8,128)(2,1)S(1)} all-to-all(bf16[24,32,512]{2,1,0:T(8,128)(2,1)S(1)} %bitcast.15), channel_id=1, replica_groups=mesh['z'=12,'h'=2,'x'=4,'y'=4,'c'=2] {'z','h'}, dimensions={0} | all-to-all | bytes 1572864 | tf_op jit(solution)/shard_map/all_to_all | solution.py:52
  111.4 0.1 convert_reduce_fusion
  111.5 0.0 copy-done.2
  111.5 0.0 copy-done.3
  111.5 0.7 divide_convert_fusion
  112.2 18.2 %all_to_all.41 = bf16[8,32,512]{2,1,0:T(8,128)(2,1)S(1)} all-to-all(bf16[8,32,512]{2,1,0:T(8,128)(2,1)S(1)} %broadcast_in_dim.5), channel_id=1, replica_groups=mesh['z'=12,'h'=2,'x'=4,'y'=4,'c'=2] {'y','c'}, dimensions={0} | all-to-all | bytes 524288 | tf_op jit(solution)/shard_map/all_to_all | solution.py:61
  130.4 1.3 convolution_convert_fusion
  (3 shorter events, 0.1 us)
Async XLA Ops:
  0.6 3.2 %copy-start = (bf16[1024,512]{1,0:T(8,128)(2,1)S(1)}, bf16[1024,512]{1,0:T(8,128)(2,1)}, u32[]{:S(2)}) copy-start(bf16[1024,512]{1,0:T(8,128)(2,1)} %param.7) | copy-start | bytes 3145732
  2.4 1.3 %copy-start.1 = (bf16[256,1024]{1,0:T(8,128)(2,1)S(1)}, bf16[256,1024]{1,0:T(8,128)(2,1)}, u32[]{:S(2)}) copy-start(bf16[256,1024]{1,0:T(8,128)(2,1)} %param.5) | copy-start | bytes 1572868
  44.9 22.8 %all-to-all-start = ((bf16[4,768,256]{2,1,0:T(8,128)(2,1)}), bf16[4,768,256]{2,1,0:T(8,128)(2,1)S(1)}, u32[]{:S(2)}, u32[]{:S(2)}) async-start(bf16[4,768,256]{2,1,0:T(8,128)(2,1)} %bitcast.18), calls=%async_computation | async-start | bytes 3145728 | tf_op jit(solution)/shard_map/all_to_all | solution.py:37
  48.5 19.3 %collective-permute-start = (bf16[4,128,512]{2,1,0:T(8,128)(2,1)S(1)}, bf16[4,128,512]{2,1,0:T(8,128)(2,1)}, u32[]{:S(2)}, u32[]{:S(2)}) collective-permute-start(bf16[4,128,512]{2,1,0:T(8,128)(2,1)S(1)} %bitcast.16), channel_id=1, source_target_pairs={{0,1},{1,0},{2,3},{3,2},{4,5},{5,4},{6,7},{7,6},{8,9},{9,8},{10,11... | collective-permute-start | bytes 1572872 | tf_op jit(solution)/shard_map/ppermute | solution.py:42
  69.8 41.7 %copy-start.2 = (f32[32,512]{1,0:T(8,128)S(1)}, f32[32,512]{1,0:T(8,128)}, u32[]{:S(2)}) copy-start(f32[32,512]{1,0:T(8,128)} %param.9) | copy-start | bytes 196612
  69.8 41.7 %copy-start.3 = (f32[32,512]{1,0:T(8,128)S(1)}, f32[32,512]{1,0:T(8,128)}, u32[]{:S(2)}) copy-start(f32[32,512]{1,0:T(8,128)} %param.8) | copy-start | bytes 196612

commit v2 on v1

--- a/solution.py
+++ b/solution.py
@@ -9,19 +9,69 @@
 AXES = ("z", "h", "x", "y", "c")
 SIZES = (12, 2, 4, 4, 2)
 SWAP = ((0, 1), (1, 0))
+NEAR = ((0, 1), (1, 0), (2, 3), (3, 2))
+FAR = ((0, 3), (3, 0), (1, 2), (2, 1))
+RING = 4
 
 
-def project(grad_ref, mine_ref, other_ref, out_ref):
+def near(x):
+    return x + 1 - 2 * lax.rem(x, 2)
+
+
+def turn(grad_ref, keep_ref, near_ref, far_ref, turned):
+    me = lax.axis_index("x")
+    for block in range(grad_ref.shape[1] // 128):
+        flipped = grad_ref[:, block * 128 : (block + 1) * 128].T
+        for x in range(RING):
+            turned[x, block * 32 : (block + 1) * 32, :] = flipped[x * 32 : (x + 1) * 32]
+    width = keep_ref.shape[0]
+    keep_ref[...] = turned[me]
+    near_ref[:width] = turned[near(me)]
+    far_ref[:width] = turned[RING - 1 - me]
+    across = RING - 1 - near(me)
+    near_ref[width:] = turned[across, : width // 2, :]
+    far_ref[width:] = turned[across, width // 2 :, :]
+
+
+def project(keep_ref, near_ref, far_ref, left_ref, right_ref, mine_ref, other_ref, out_ref):
+    me = lax.axis_index("x")
     first = lax.axis_index("c") == 0
+    width = keep_ref.shape[0]
+    across = jnp.concatenate([left_ref[...], right_ref[...]], axis=0)
+    sources = (
+        (keep_ref[...], me),
+        (near_ref[:width], near(me)),
+        (far_ref[:width], RING - 1 - me),
+        (across, RING - 1 - near(me)),
+    )
     total = None
-    for x in range(grad_ref.shape[0]):
+    for grad, x in sources:
         mine, other = mine_ref[x], other_ref[x]
         low = jnp.where(first, mine, other)
         high = jnp.where(first, other, mine)
         reduced = jnp.concatenate([low, high], axis=0)
-        term = jnp.dot(grad_ref[x], reduced, preferred_element_type=jnp.float32)
+        term = jnp.dot(grad, reduced, preferred_element_type=jnp.float32)
         total = term if total is None else total + term
     out_ref[...] = total.astype(out_ref.dtype)
+
+
+def share(partial_ref, copies_ref):
+    reduced = jnp.sum(partial_ref[...].astype(jnp.float32), axis=0).astype(copies_ref.dtype)
+    for i in range(copies_ref.shape[0]):
+        copies_ref[i] = reduced
+
+
+def whole(kernel, ins, outs, scratch=(), flops=0):
+    spec = pl.BlockSpec(memory_space=pltpu.VMEM)
+    return pl.pallas_call(
+        kernel,
+        out_shape=outs,
+        in_specs=[spec] * ins,
+        out_specs=jax.tree.map(lambda _: spec, outs),
+        scratch_shapes=scratch,
+        compiler_params=pltpu.CompilerParams(vmem_limit_bytes=24 * 1024 * 1024),
+        cost_estimate=pl.CostEstimate(flops=flops, bytes_accessed=4 << 20, transcendentals=0),
+    )
 
 
 def shards(hidden_in, grad_out, basis, first_moment, second_moment):
@@ -30,25 +80,29 @@
     rank = basis.shape[1]
     tokens = hidden_in.shape[0]
     piece = tokens // 8
-    turned = grad_out.T.reshape(24, 4, rows, tokens).transpose(1, 0, 2, 3).reshape(4, 24 * rows, tokens)
+    width = 24 * rows
+    shape = jax.ShapeDtypeStruct
+    more = shape((width + width // 2, tokens), bf16)
+    keep, to_near, to_far = whole(
+        turn, 1, [shape((width, tokens), bf16), more, more], [pltpu.VMEM((RING, width, tokens), bf16)]
+    )(grad_out)
+    from_near = lax.ppermute(to_near, "x", NEAR)
+    from_far = lax.ppermute(to_far, "x", FAR)
 
     partial = jnp.dot(hidden_in, basis, preferred_element_type=f32).astype(bf16)
-    partial, turned = lax.optimization_barrier((partial, turned))
-    spread = lax.all_to_all(turned, "x", 0, 0, tiled=True)
     partial = lax.all_to_all(partial, ("c", "y"), 0, 0, tiled=True).reshape(8, piece, rank)
-    reduced = jnp.sum(partial.astype(f32), axis=0).astype(bf16)
-    copies = jnp.broadcast_to(reduced[None], (16, piece, rank)).reshape(-1, rank)
+    partial, from_near, from_far = lax.optimization_barrier((partial, from_near, from_far))
+
+    left = lax.ppermute(from_near[width:], "x", FAR)
+    right = lax.ppermute(from_far[width:], "x", NEAR)
+    copies = whole(share, 1, shape((16, piece, rank), bf16))(partial).reshape(-1, rank)
     mine = lax.all_to_all(copies, ("x", "y"), 0, 0, tiled=True).reshape(4, 4 * piece, rank)
+    mine, left, right = lax.optimization_barrier((mine, left, right))
     other = lax.ppermute(mine, "c", SWAP)
 
-    part = pl.pallas_call(
-        project,
-        out_shape=jax.ShapeDtypeStruct((24 * rows, rank), bf16),
-        in_specs=[pl.BlockSpec(memory_space=pltpu.VMEM)] * 3,
-        out_specs=pl.BlockSpec(memory_space=pltpu.VMEM),
-        compiler_params=pltpu.CompilerParams(vmem_limit_bytes=32 * 1024 * 1024),
-        cost_estimate=pl.CostEstimate(flops=2 * 24 * rows * 4 * tokens * rank, bytes_accessed=4 << 20, transcendentals=0),
-    )(spread, mine, other)
+    part = whole(project, 7, shape((width, rank), bf16), flops=2 * width * 4 * tokens * rank)(
+        keep, from_near, from_far, left, right, mine, other
+    )
     part = lax.all_to_all(part, ("z", "h"), 0, 0, tiled=True).reshape(24, rows, rank)
     projected = jnp.sum(part.astype(f32), axis=0)
 

time: 132 us -> 120 us (0.909)
  blocking collectives: 100 us -> 78.3 us
  starting transfers between devices: 6.93 us -> 23.5 us
  waiting for transfers between devices: 15.9 us -> 10.2 us
  local copies, waits for them, and re-layouts: 3.21 us -> 1.56 us
    all_to_all x1 -> x0, blocking collectives: 18.6 us -> none  [shards(): lax.all_to_all(copies, ('x', 'y'), 0, 0, tiled=True)]
    ppermute x0 -> x4, starting transfers between devices: none -> 14.6 us  [the longest x1 3.95 us: shards(): from_near = lax.ppermute(to_near, 'x', NEAR)]
    all_to_all x1, waiting for transfers between devices: 15.9 us -> 1.93 us  [shards(): lax.all_to_all(copies, ('x', 'y'), 0, 0, tiled=True)]
    ppermute x0 -> x4, waiting for transfers between devices: none -> 6.79 us  [the longest x1 5.56 us: shards(): right = lax.ppermute(from_far[width:], 'x', NEAR)]
    all_to_all x1, blocking collectives: 22 us -> 18.1 us  [shards(): lax.all_to_all(partial, ('c', 'y'), 0, 0, tiled=True)]
    all_to_all x1, blocking collectives: 41.6 us -> 44.9 us  [shards(): lax.all_to_all(part, ('z', 'h'), 0, 0, tiled=True).reshape(24, rows, rank)]
    all_to_all x1, blocking collectives: 18.2 us -> 15.2 us  [shards(): grouped = lax.all_to_all(copies, ('y', 'c'), 0, 0, tiled=True)]
    all_to_all x1, starting transfers between devices: 3.56 us -> 5.22 us  [shards(): lax.all_to_all(copies, ('x', 'y'), 0, 0, tiled=True)]
  transfers between devices with their start and end apart: 2 -> 6, of which waited for: 1 -> 4; matrix products, arithmetic and copies ran while one was open for 0% -> 0% of each run, Pallas kernels for 0% -> 0%
where the time goes in v2:
time: 120 us; the launch traced here: 119 us
  blocking collectives  78.3 us (65%)
  starting transfers between devices  23.5 us (20%)
  waiting for transfers between devices  10.2 us (8%)
  Pallas kernels  2.35 us (2%)
  matrix products  1.7 us (1%)
  local copies, waits for them, and re-layouts  1.56 us (1%)
    all_to_all x1, blocking collectives, shards(): lax.all_to_all(part, ('z', 'h'), 0, 0, tiled=True).reshape(24, rows, rank)  44.9 us
    all_to_all x1, blocking collectives, shards(): lax.all_to_all(partial, ('c', 'y'), 0, 0, tiled=True)  18.1 us
    all_to_all x1, blocking collectives, shards(): grouped = lax.all_to_all(copies, ('y', 'c'), 0, 0, tiled=True)  15.2 us
    ppermute x1, waiting for transfers between devices, shards(): right = lax.ppermute(from_far[width:], 'x', NEAR)  5.56 us
    all_to_all x1, starting transfers between devices, shards(): lax.all_to_all(copies, ('x', 'y'), 0, 0, tiled=True)  5.22 us
    ppermute x1, starting transfers between devices, shards(): from_near = lax.ppermute(to_near, 'x', NEAR)  3.95 us
    ppermute x1, starting transfers between devices, shards(): from_far = lax.ppermute(to_far, 'x', FAR)  3.72 us
    ppermute x1, starting transfers between devices, shards(): left = lax.ppermute(from_near[width:], 'x', FAR)  3.7 us
  transfers between devices with their start and end apart: 6, of which 4 were waited for; matrix products, arithmetic and copies ran while one was open for 0% of the time, Pallas kernels for 0%

profile of v2, /device:TPU:1, one launch (start us, length us, event | category | flops | bytes accessed | tf_op | source)
XLA Modules:
  0.0 119.2 jit_solution(6177855558394587728)
XLA Ops:
  0.6 0.0 copy-start
  0.6 0.0 copy-start.1
  0.7 1.5 %copy-done.1 = bf16[256,3072]{1,0:T(8,128)(2,1)S(1)} copy-done((bf16[256,3072]{1,0:T(8,128)(2,1)S(1)}, bf16[256,3072]{1,0:T(8,128)(2,1)}, u32[]{:S(2)}) %copy-start.1) | copy-done | bytes 1572888
  2.1 0.0 copy-start.2
  2.1 0.5 shard_map.76
  2.7 3.9 %collective-permute-start = (bf16[1152,256]{1,0:T(8,128)(2,1)S(1)}, bf16[1152,256]{1,0:T(8,128)(2,1)S(1)}, u32[]{:S(2)}, u32[]{:S(2)}) collective-permute-start(bf16[1152,256]{1,0:T(8,128)(2,1)S(1)} %get-tuple-element.13), channel_id=1, source_target_pairs={{0,8},{8,0},{16,24},{24,16},{1,9},{9,1},{17,25},{25,17},{2,10},{10... | collective-permute-start | bytes 1769480 | tf_op jit(solution)/shard_map/ppermute | solution.py:89
  6.6 3.7 %collective-permute-start.1 = (bf16[1152,256]{1,0:T(8,128)(2,1)S(1)}, bf16[1152,256]{1,0:T(8,128)(2,1)S(1)}, u32[]{:S(2)}, u32[]{:S(2)}) collective-permute-start(bf16[1152,256]{1,0:T(8,128)(2,1)S(1)} %get-tuple-element.14), channel_id=1, source_target_pairs={{0,24},{24,0},{8,16},{16,8},{1,25},{25,1},{9,17},{17,9},{2,26},{26... | collective-permute-start | bytes 1769480 | tf_op jit(solution)/shard_map/ppermute | solution.py:90
  10.4 0.0 copy-done
  10.4 0.0 copy-done.2
  10.4 0.4 convolution_convert_fusion.1
  10.8 18.1 %all_to_all.33.partial_ref = bf16[8,32,512]{2,1,0:T(8,128)(2,1)S(1)} all-to-all(bf16[8,32,512]{2,1,0:T(8,128)(2,1)S(1)} %bitcast.13), channel_id=1, replica_groups=mesh['z'=12,'h'=2,'x'=4,'y'=4,'c'=2] {'c','y'}, dimensions={0} | all-to-all | bytes 524288 | tf_op jit(solution)/shard_map/all_to_all | solution.py:93
  29.0 0.0 collective-permute-done.near_ref
  29.0 0.0 collective-permute-done.1.far_ref
  29.0 0.9 shard_map.77
  29.8 5.2 %all-to-all-start.1 = ((bf16[16,32,512]{2,1,0:T(8,128)(2,1)}), bf16[16,32,512]{2,1,0:T(8,128)(2,1)S(1)}, u32[]{:S(2)}, u32[]{:S(2)}) async-start(bf16[16,32,512]{2,1,0:T(8,128)(2,1)} %shard_map.77), calls=%async_computation.1 | async-start | bytes 1048576 | tf_op jit(solution)/shard_map/all_to_all | solution.py:99
  35.1 3.3 %collective-permute-start.3 = (bf16[384,256]{1,0:T(8,128)(2,1)S(1)}, bf16[384,256]{1,0:T(8,128)(2,1)S(1)}, u32[]{:S(2)}, u32[]{:S(2)}) collective-permute-start(bf16[384,256]{1,0:T(8,128)(2,1)S(1)} %slice.7), channel_id=1, source_target_pairs={{0,8},{8,0},{16,24},{24,16},{1,9},{9,1},{17,25},{25,17},{2,10},{10... | collective-permute-start | bytes 589832 | tf_op jit(solution)/shard_map/ppermute | solution.py:97
  38.4 3.7 %collective-permute-start.2 = (bf16[384,256]{1,0:T(8,128)(2,1)S(1)}, bf16[384,256]{1,0:T(8,128)(2,1)S(1)}, u32[]{:S(2)}, u32[]{:S(2)}) collective-permute-start(bf16[384,256]{1,0:T(8,128)(2,1)S(1)} %slice.6), channel_id=1, source_target_pairs={{0,24},{24,0},{8,16},{16,8},{1,25},{25,1},{9,17},{17,9},{2,26},{26... | collective-permute-start | bytes 589832 | tf_op jit(solution)/shard_map/ppermute | solution.py:96
  42.1 5.6 %collective-permute-done.3.right_ref = bf16[384,256]{1,0:T(8,128)(2,1)S(1)} collective-permute-done((bf16[384,256]{1,0:T(8,128)(2,1)S(1)}, bf16[384,256]{1,0:T(8,128)(2,1)S(1)}, u32[]{:S(2)}, u32[]{:S(2)}) %collective-permute-start.3) | collective-permute-done | bytes 196640 | tf_op jit(solution)/shard_map/ppermute | solution.py:97
  47.6 1.2 %collective-permute-done.2.left_ref = bf16[384,256]{1,0:T(8,128)(2,1)S(1)} collective-permute-done((bf16[384,256]{1,0:T(8,128)(2,1)S(1)}, bf16[384,256]{1,0:T(8,128)(2,1)S(1)}, u32[]{:S(2)}, u32[]{:S(2)}) %collective-permute-start.2) | collective-permute-done | bytes 196640 | tf_op jit(solution)/shard_map/ppermute | solution.py:96
  48.9 1.9 %all-to-all-done.1 = bf16[16,32,512]{2,1,0:T(8,128)(2,1)S(1)} async-done(((bf16[16,32,512]{2,1,0:T(8,128)(2,1)}), bf16[16,32,512]{2,1,0:T(8,128)(2,1)S(1)}, u32[]{:S(2)}, u32[]{:S(2)}) %all-to-all-start.1) | async-done | bytes 524320 | tf_op jit(solution)/shard_map/all_to_all | solution.py:99
  50.8 3.6 %collective-permute-start.4 = (bf16[4,128,512]{2,1,0:T(8,128)(2,1)S(1)}, bf16[4,128,512]{2,1,0:T(8,128)(2,1)S(1)}, u32[]{:S(2)}, u32[]{:S(2)}) collective-permute-start(bf16[4,128,512]{2,1,0:T(8,128)(2,1)S(1)} %bitcast.10), channel_id=1, source_target_pairs={{0,1},{1,0},{2,3},{3,2},{4,5},{5,4},{6,7},{7,6},{8,9},{9,8},{10,11... | collective-permute-start | bytes 1572872 | tf_op jit(solution)/shard_map/ppermute | solution.py:101
  54.4 1.5 %collective-permute-done.4.other_ref = bf16[4,128,512]{2,1,0:T(8,128)(2,1)S(1)} collective-permute-done((bf16[4,128,512]{2,1,0:T(8,128)(2,1)S(1)}, bf16[4,128,512]{2,1,0:T(8,128)(2,1)S(1)}, u32[]{:S(2)}, u32[]{:S(2)}) %collective-permute-start.4) | collective-permute-done | bytes 524320 | tf_op jit(solution)/shard_map/ppermute | solution.py:101
  55.9 1.0 shard_map.78
  56.9 0.0 copy-start.3
  56.9 0.0 copy-start.4
  56.9 44.9 %all_to_all.34 = bf16[24,32,512]{2,1,0:T(8,128)(2,1)S(1)} all-to-all(bf16[24,32,512]{2,1,0:T(8,128)(2,1)S(1)} %bitcast.9), channel_id=1, replica_groups=mesh['z'=12,'h'=2,'x'=4,'y'=4,'c'=2] {'z','h'}, dimensions={0} | all-to-all | bytes 1572864 | tf_op jit(solution)/shard_map/all_to_all | solution.py:106
  101.9 0.1 convert_reduce_fusion
  102.0 0.0 copy-done.3
  102.0 0.0 copy-done.4
  102.0 0.7 divide_convert_fusion
  102.7 15.2 %all_to_all.35 = bf16[8,32,512]{2,1,0:T(8,128)(2,1)S(1)} all-to-all(bf16[8,32,512]{2,1,0:T(8,128)(2,1)S(1)} %broadcast_in_dim.2), channel_id=1, replica_groups=mesh['z'=12,'h'=2,'x'=4,'y'=4,'c'=2] {'y','c'}, dimensions={0} | all-to-all | bytes 524288 | tf_op jit(solution)/shard_map/all_to_all | solution.py:115
  117.9 1.3 %convolution_convert_fusion = bf16[256,1024]{1,0:T(8,128)(2,1)} fusion(bf16[256,512]{1,0:T(8,128)(2,1)S(1)} %bitcast.12, bf16[1024,512]{1,0:T(8,128)(2,1)S(1)} %copy-done), kind=kOutput, calls=%fused_computation.1 | convolution fusion | flops 268697600 | bytes 1835008 | tf_op jit(solution)/shard_map/dot_general | solution.py:116
  (3 shorter events, 0.0 us)
Async XLA Ops:
  0.6 9.7 %copy-start = (bf16[1024,512]{1,0:T(8,128)(2,1)S(1)}, bf16[1024,512]{1,0:T(8,128)(2,1)}, u32[]{:S(2)}) copy-start(bf16[1024,512]{1,0:T(8,128)(2,1)} %param.7) | copy-start | bytes 3145732
  0.6 1.5 %copy-start.1 = (bf16[256,3072]{1,0:T(8,128)(2,1)S(1)}, bf16[256,3072]{1,0:T(8,128)(2,1)}, u32[]{:S(2)}) copy-start(bf16[256,3072]{1,0:T(8,128)(2,1)} %grad_ref.1) | copy-start | bytes 4718596
  2.1 8.2 %copy-start.2 = (bf16[256,1024]{1,0:T(8,128)(2,1)S(1)}, bf16[256,1024]{1,0:T(8,128)(2,1)}, u32[]{:S(2)}) copy-start(bf16[256,1024]{1,0:T(8,128)(2,1)} %param.5) | copy-start | bytes 1572868
  2.7 26.3 %collective-permute-start = (bf16[1152,256]{1,0:T(8,128)(2,1)S(1)}, bf16[1152,256]{1,0:T(8,128)(2,1)S(1)}, u32[]{:S(2)}, u32[]{:S(2)}) collective-permute-start(bf16[1152,256]{1,0:T(8,128)(2,1)S(1)} %get-tuple-element.13), channel_id=1, source_target_pairs={{0,8},{8,0},{16,24},{24,16},{1,9},{9,1},{17,25},{25,17},{2,10},{10... | collective-permute-start | bytes 1769480 | tf_op jit(solution)/shard_map/ppermute | solution.py:89
  6.6 22.3 %collective-permute-start.1 = (bf16[1152,256]{1,0:T(8,128)(2,1)S(1)}, bf16[1152,256]{1,0:T(8,128)(2,1)S(1)}, u32[]{:S(2)}, u32[]{:S(2)}) collective-permute-start(bf16[1152,256]{1,0:T(8,128)(2,1)S(1)} %get-tuple-element.14), channel_id=1, source_target_pairs={{0,24},{24,0},{8,16},{16,8},{1,25},{25,1},{9,17},{17,9},{2,26},{26... | collective-permute-start | bytes 1769480 | tf_op jit(solution)/shard_map/ppermute | solution.py:90
  29.8 21.0 %all-to-all-start.1 = ((bf16[16,32,512]{2,1,0:T(8,128)(2,1)}), bf16[16,32,512]{2,1,0:T(8,128)(2,1)S(1)}, u32[]{:S(2)}, u32[]{:S(2)}) async-start(bf16[16,32,512]{2,1,0:T(8,128)(2,1)} %shard_map.77), calls=%async_computation.1 | async-start | bytes 1048576 | tf_op jit(solution)/shard_map/all_to_all | solution.py:99
  35.1 12.5 %collective-permute-start.3 = (bf16[384,256]{1,0:T(8,128)(2,1)S(1)}, bf16[384,256]{1,0:T(8,128)(2,1)S(1)}, u32[]{:S(2)}, u32[]{:S(2)}) collective-permute-start(bf16[384,256]{1,0:T(8,128)(2,1)S(1)} %slice.7), channel_id=1, source_target_pairs={{0,8},{8,0},{16,24},{24,16},{1,9},{9,1},{17,25},{25,17},{2,10},{10... | collective-permute-start | bytes 589832 | tf_op jit(solution)/shard_map/ppermute | solution.py:97
  38.4 10.5 %collective-permute-start.2 = (bf16[384,256]{1,0:T(8,128)(2,1)S(1)}, bf16[384,256]{1,0:T(8,128)(2,1)S(1)}, u32[]{:S(2)}, u32[]{:S(2)}) collective-permute-start(bf16[384,256]{1,0:T(8,128)(2,1)S(1)} %slice.6), channel_id=1, source_target_pairs={{0,24},{24,0},{8,16},{16,8},{1,25},{25,1},{9,17},{17,9},{2,26},{26... | collective-permute-start | bytes 589832 | tf_op jit(solution)/shard_map/ppermute | solution.py:96
  50.8 5.1 %collective-permute-start.4 = (bf16[4,128,512]{2,1,0:T(8,128)(2,1)S(1)}, bf16[4,128,512]{2,1,0:T(8,128)(2,1)S(1)}, u32[]{:S(2)}, u32[]{:S(2)}) collective-permute-start(bf16[4,128,512]{2,1,0:T(8,128)(2,1)S(1)} %bitcast.10), channel_id=1, source_target_pairs={{0,1},{1,0},{2,3},{3,2},{4,5},{5,4},{6,7},{7,6},{8,9},{9,8},{10,11... | collective-permute-start | bytes 1572872 | tf_op jit(solution)/shard_map/ppermute | solution.py:101
  56.9 45.1 %copy-start.3 = (f32[32,512]{1,0:T(8,128)S(1)}, f32[32,512]{1,0:T(8,128)}, u32[]{:S(2)}) copy-start(f32[32,512]{1,0:T(8,128)} %param.9) | copy-start | bytes 196612
  56.9 45.1 %copy-start.4 = (f32[32,512]{1,0:T(8,128)S(1)}, f32[32,512]{1,0:T(8,128)}, u32[]{:S(2)}) copy-start(f32[32,512]{1,0:T(8,128)} %param.8) | copy-start | bytes 196612

commit v3 on v2

--- a/solution.py
+++ b/solution.py
@@ -111,8 +111,9 @@
     first_hat = new_first / (1.0 - 0.9**STEP)
     second_hat = new_second / (1.0 - 0.999**STEP)
     direction = (first_hat / (jnp.sqrt(second_hat) + 1e-08)).astype(bf16)
-    copies = jnp.broadcast_to(direction[None], (8, rows, rank)).reshape(-1, rank)
-    grouped = lax.all_to_all(copies, ("y", "c"), 0, 0, tiled=True)
+    copies = jnp.broadcast_to(direction[None], (4, rows, rank)).reshape(-1, rank)
+    grouped = lax.all_to_all(copies, "y", 0, 0, tiled=True).reshape(4, rows, rank)
+    grouped = lax.all_gather(grouped, "c", axis=1, tiled=False).reshape(8 * rows, rank)
     update = lax.dot_general(grouped, basis, (((1,), (1,)), ((), ())), preferred_element_type=f32)
     return (new_first, new_second, update.astype(bf16).reshape(8, rows, -1))
 

time: 120 us -> 119 us (level)
  blocking collectives: 78.3 us -> 77.1 us
    all_to_all x1, blocking collectives: 15.2 us -> 7.16 us  [shards(): lax.all_to_all(copies, 'y', 0, 0, tiled=True).reshape(4, rows, rank)]
    all_gather x0 -> x1, blocking collectives: none -> 6.86 us  [shards(): lax.all_gather(grouped, 'c', axis=1, tiled=False).reshape(8 * rows, rank)]
where the time goes in v3:
time: 119 us; the launch traced here: 118 us
  blocking collectives  77.1 us (65%)
  starting transfers between devices  23.5 us (20%)
  waiting for transfers between devices  10.2 us (9%)
  Pallas kernels  2.35 us (2%)
  matrix products  1.7 us (1%)
  local copies, waits for them, and re-layouts  1.55 us (1%)
    all_to_all x1, blocking collectives, shards(): lax.all_to_all(part, ('z', 'h'), 0, 0, tiled=True).reshape(24, rows, rank)  44.9 us
    all_to_all x1, blocking collectives, shards(): lax.all_to_all(partial, ('c', 'y'), 0, 0, tiled=True)  18.1 us
    all_to_all x1, blocking collectives, shards(): lax.all_to_all(copies, 'y', 0, 0, tiled=True).reshape(4, rows, rank)  7.16 us
    all_gather x1, blocking collectives, shards(): lax.all_gather(grouped, 'c', axis=1, tiled=False).reshape(8 * rows, rank)  6.86 us
    ppermute x1, waiting for transfers between devices, shards(): right = lax.ppermute(from_far[width:], 'x', NEAR)  5.56 us
    all_to_all x1, starting transfers between devices, shards(): lax.all_to_all(copies, ('x', 'y'), 0, 0, tiled=True)  5.22 us
    ppermute x1, starting transfers between devices, shards(): from_near = lax.ppermute(to_near, 'x', NEAR)  3.95 us
    ppermute x1, starting transfers between devices, shards(): from_far = lax.ppermute(to_far, 'x', FAR)  3.72 us
  transfers between devices with their start and end apart: 6, of which 4 were waited for; matrix products, arithmetic and copies ran while one was open for 0% of the time, Pallas kernels for 0%

profile of v3, /device:TPU:1, one launch (start us, length us, event | category | flops | bytes accessed | tf_op | source)
XLA Modules:
  0.0 118.0 jit_solution(16811709589855962505)
XLA Ops:
  0.6 0.0 copy-start
  0.6 0.0 copy-start.1
  0.7 1.5 %copy-done.1 = bf16[256,3072]{1,0:T(8,128)(2,1)S(1)} copy-done((bf16[256,3072]{1,0:T(8,128)(2,1)S(1)}, bf16[256,3072]{1,0:T(8,128)(2,1)}, u32[]{:S(2)}) %copy-start.1) | copy-done | bytes 1572888
  2.1 0.5 shard_map.76
  2.7 3.9 %collective-permute-start = (bf16[1152,256]{1,0:T(8,128)(2,1)S(1)}, bf16[1152,256]{1,0:T(8,128)(2,1)S(1)}, u32[]{:S(2)}, u32[]{:S(2)}) collective-permute-start(bf16[1152,256]{1,0:T(8,128)(2,1)S(1)} %get-tuple-element.13), channel_id=1, source_target_pairs={{0,8},{8,0},{16,24},{24,16},{1,9},{9,1},{17,25},{25,17},{2,10},{10... | collective-permute-start | bytes 1769480 | tf_op jit(solution)/shard_map/ppermute | solution.py:89
  6.6 3.7 %collective-permute-start.1 = (bf16[1152,256]{1,0:T(8,128)(2,1)S(1)}, bf16[1152,256]{1,0:T(8,128)(2,1)S(1)}, u32[]{:S(2)}, u32[]{:S(2)}) collective-permute-start(bf16[1152,256]{1,0:T(8,128)(2,1)S(1)} %get-tuple-element.14), channel_id=1, source_target_pairs={{0,24},{24,0},{8,16},{16,8},{1,25},{25,1},{9,17},{17,9},{2,26},{26... | collective-permute-start | bytes 1769480 | tf_op jit(solution)/shard_map/ppermute | solution.py:90
  10.4 0.0 copy-done
  10.4 0.0 copy-done.2
  10.4 0.4 convolution_convert_fusion.1
  10.8 18.1 %all_to_all.30.partial_ref = bf16[8,32,512]{2,1,0:T(8,128)(2,1)S(1)} all-to-all(bf16[8,32,512]{2,1,0:T(8,128)(2,1)S(1)} %bitcast.13), channel_id=1, replica_groups=mesh['z'=12,'h'=2,'x'=4,'y'=4,'c'=2] {'c','y'}, dimensions={0} | all-to-all | bytes 524288 | tf_op jit(solution)/shard_map/all_to_all | solution.py:93
  29.0 0.0 collective-permute-done.near_ref
  29.0 0.0 collective-permute-done.1.far_ref
  29.0 0.9 shard_map.77
  29.8 5.2 %all-to-all-start.1 = ((bf16[16,32,512]{2,1,0:T(8,128)(2,1)}), bf16[16,32,512]{2,1,0:T(8,128)(2,1)S(1)}, u32[]{:S(2)}, u32[]{:S(2)}) async-start(bf16[16,32,512]{2,1,0:T(8,128)(2,1)} %shard_map.77), calls=%async_computation.1 | async-start | bytes 1048576 | tf_op jit(solution)/shard_map/all_to_all | solution.py:99
  35.1 3.3 %collective-permute-start.3 = (bf16[384,256]{1,0:T(8,128)(2,1)S(1)}, bf16[384,256]{1,0:T(8,128)(2,1)S(1)}, u32[]{:S(2)}, u32[]{:S(2)}) collective-permute-start(bf16[384,256]{1,0:T(8,128)(2,1)S(1)} %slice.7), channel_id=1, source_target_pairs={{0,8},{8,0},{16,24},{24,16},{1,9},{9,1},{17,25},{25,17},{2,10},{10... | collective-permute-start | bytes 589832 | tf_op jit(solution)/shard_map/ppermute | solution.py:97
  38.4 3.7 %collective-permute-start.2 = (bf16[384,256]{1,0:T(8,128)(2,1)S(1)}, bf16[384,256]{1,0:T(8,128)(2,1)S(1)}, u32[]{:S(2)}, u32[]{:S(2)}) collective-permute-start(bf16[384,256]{1,0:T(8,128)(2,1)S(1)} %slice.6), channel_id=1, source_target_pairs={{0,24},{24,0},{8,16},{16,8},{1,25},{25,1},{9,17},{17,9},{2,26},{26... | collective-permute-start | bytes 589832 | tf_op jit(solution)/shard_map/ppermute | solution.py:96
  42.1 5.6 %collective-permute-done.3.right_ref = bf16[384,256]{1,0:T(8,128)(2,1)S(1)} collective-permute-done((bf16[384,256]{1,0:T(8,128)(2,1)S(1)}, bf16[384,256]{1,0:T(8,128)(2,1)S(1)}, u32[]{:S(2)}, u32[]{:S(2)}) %collective-permute-start.3) | collective-permute-done | bytes 196640 | tf_op jit(solution)/shard_map/ppermute | solution.py:97
  47.6 1.2 %collective-permute-done.2.left_ref = bf16[384,256]{1,0:T(8,128)(2,1)S(1)} collective-permute-done((bf16[384,256]{1,0:T(8,128)(2,1)S(1)}, bf16[384,256]{1,0:T(8,128)(2,1)S(1)}, u32[]{:S(2)}, u32[]{:S(2)}) %collective-permute-start.2) | collective-permute-done | bytes 196640 | tf_op jit(solution)/shard_map/ppermute | solution.py:96
  48.9 1.9 %all-to-all-done.1 = bf16[16,32,512]{2,1,0:T(8,128)(2,1)S(1)} async-done(((bf16[16,32,512]{2,1,0:T(8,128)(2,1)}), bf16[16,32,512]{2,1,0:T(8,128)(2,1)S(1)}, u32[]{:S(2)}, u32[]{:S(2)}) %all-to-all-start.1) | async-done | bytes 524320 | tf_op jit(solution)/shard_map/all_to_all | solution.py:99
  50.8 3.6 %collective-permute-start.4 = (bf16[4,128,512]{2,1,0:T(8,128)(2,1)S(1)}, bf16[4,128,512]{2,1,0:T(8,128)(2,1)S(1)}, u32[]{:S(2)}, u32[]{:S(2)}) collective-permute-start(bf16[4,128,512]{2,1,0:T(8,128)(2,1)S(1)} %bitcast.10), channel_id=1, source_target_pairs={{0,1},{1,0},{2,3},{3,2},{4,5},{5,4},{6,7},{7,6},{8,9},{9,8},{10,11... | collective-permute-start | bytes 1572872 | tf_op jit(solution)/shard_map/ppermute | solution.py:101
  54.4 1.5 %collective-permute-done.4.other_ref = bf16[4,128,512]{2,1,0:T(8,128)(2,1)S(1)} collective-permute-done((bf16[4,128,512]{2,1,0:T(8,128)(2,1)S(1)}, bf16[4,128,512]{2,1,0:T(8,128)(2,1)S(1)}, u32[]{:S(2)}, u32[]{:S(2)}) %collective-permute-start.4) | collective-permute-done | bytes 524320 | tf_op jit(solution)/shard_map/ppermute | solution.py:101
  55.9 1.0 shard_map.78
  56.9 0.0 copy-start.3
  56.9 0.0 copy-start.4
  56.9 44.9 %all_to_all.31 = bf16[24,32,512]{2,1,0:T(8,128)(2,1)S(1)} all-to-all(bf16[24,32,512]{2,1,0:T(8,128)(2,1)S(1)} %bitcast.9), channel_id=1, replica_groups=mesh['z'=12,'h'=2,'x'=4,'y'=4,'c'=2] {'z','h'}, dimensions={0} | all-to-all | bytes 1572864 | tf_op jit(solution)/shard_map/all_to_all | solution.py:106
  101.9 0.1 convert_reduce_fusion
  102.0 0.0 copy-done.3
  102.0 0.0 copy-done.4
  102.0 0.7 divide_convert_fusion
  102.7 7.2 %all_to_all.32 = bf16[4,32,512]{2,1,0:T(8,128)(2,1)S(1)} all-to-all(bf16[4,32,512]{2,1,0:T(8,128)(2,1)S(1)} %broadcast_in_dim.2), channel_id=1, replica_groups=mesh['z'=12,'h'=2,'x'=4,'y'=4,'c'=2] {'y'}, dimensions={0} | all-to-all | bytes 262144 | tf_op jit(solution)/shard_map/all_to_all | solution.py:115
  109.9 6.9 %all-gather = bf16[4,64,512]{2,1,0:T(8,128)(2,1)S(1)} all-gather(bf16[4,32,512]{2,1,0:T(8,128)(2,1)S(1)} %all_to_all.32), channel_id=2, replica_groups=mesh['z'=12,'h'=2,'x'=4,'y'=4,'c'=2] {'c'}, dimensions={1}, use_global_device_ids=true | all-gather | bytes 393216 | tf_op jit(solution)/shard_map/all_gather | solution.py:116
  116.7 1.3 %convolution_convert_fusion = bf16[256,1024]{1,0:T(8,128)(2,1)} fusion(bf16[256,512]{1,0:T(8,128)(2,1)S(1)} %bitcast.12, bf16[1024,512]{1,0:T(8,128)(2,1)S(1)} %copy-done), kind=kOutput, calls=%fused_computation.1 | convolution fusion | flops 268697600 | bytes 1835008 | tf_op jit(solution)/shard_map/dot_general | solution.py:117
  (4 shorter events, 0.0 us)
Async XLA Ops:
  0.6 9.7 %copy-start = (bf16[1024,512]{1,0:T(8,128)(2,1)S(1)}, bf16[1024,512]{1,0:T(8,128)(2,1)}, u32[]{:S(2)}) copy-start(bf16[1024,512]{1,0:T(8,128)(2,1)} %param.7) | copy-start | bytes 3145732
  0.6 1.5 %copy-start.1 = (bf16[256,3072]{1,0:T(8,128)(2,1)S(1)}, bf16[256,3072]{1,0:T(8,128)(2,1)}, u32[]{:S(2)}) copy-start(bf16[256,3072]{1,0:T(8,128)(2,1)} %grad_ref.1) | copy-start | bytes 4718596
  2.1 8.2 %copy-start.2 = (bf16[256,1024]{1,0:T(8,128)(2,1)S(1)}, bf16[256,1024]{1,0:T(8,128)(2,1)}, u32[]{:S(2)}) copy-start(bf16[256,1024]{1,0:T(8,128)(2,1)} %param.5) | copy-start | bytes 1572868
  2.7 26.3 %collective-permute-start = (bf16[1152,256]{1,0:T(8,128)(2,1)S(1)}, bf16[1152,256]{1,0:T(8,128)(2,1)S(1)}, u32[]{:S(2)}, u32[]{:S(2)}) collective-permute-start(bf16[1152,256]{1,0:T(8,128)(2,1)S(1)} %get-tuple-element.13), channel_id=1, source_target_pairs={{0,8},{8,0},{16,24},{24,16},{1,9},{9,1},{17,25},{25,17},{2,10},{10... | collective-permute-start | bytes 1769480 | tf_op jit(solution)/shard_map/ppermute | solution.py:89
  6.6 22.3 %collective-permute-start.1 = (bf16[1152,256]{1,0:T(8,128)(2,1)S(1)}, bf16[1152,256]{1,0:T(8,128)(2,1)S(1)}, u32[]{:S(2)}, u32[]{:S(2)}) collective-permute-start(bf16[1152,256]{1,0:T(8,128)(2,1)S(1)} %get-tuple-element.14), channel_id=1, source_target_pairs={{0,24},{24,0},{8,16},{16,8},{1,25},{25,1},{9,17},{17,9},{2,26},{26... | collective-permute-start | bytes 1769480 | tf_op jit(solution)/shard_map/ppermute | solution.py:90
  29.8 21.0 %all-to-all-start.1 = ((bf16[16,32,512]{2,1,0:T(8,128)(2,1)}), bf16[16,32,512]{2,1,0:T(8,128)(2,1)S(1)}, u32[]{:S(2)}, u32[]{:S(2)}) async-start(bf16[16,32,512]{2,1,0:T(8,128)(2,1)} %shard_map.77), calls=%async_computation.1 | async-start | bytes 1048576 | tf_op jit(solution)/shard_map/all_to_all | solution.py:99
  35.1 12.5 %collective-permute-start.3 = (bf16[384,256]{1,0:T(8,128)(2,1)S(1)}, bf16[384,256]{1,0:T(8,128)(2,1)S(1)}, u32[]{:S(2)}, u32[]{:S(2)}) collective-permute-start(bf16[384,256]{1,0:T(8,128)(2,1)S(1)} %slice.7), channel_id=1, source_target_pairs={{0,8},{8,0},{16,24},{24,16},{1,9},{9,1},{17,25},{25,17},{2,10},{10... | collective-permute-start | bytes 589832 | tf_op jit(solution)/shard_map/ppermute | solution.py:97
  38.4 10.5 %collective-permute-start.2 = (bf16[384,256]{1,0:T(8,128)(2,1)S(1)}, bf16[384,256]{1,0:T(8,128)(2,1)S(1)}, u32[]{:S(2)}, u32[]{:S(2)}) collective-permute-start(bf16[384,256]{1,0:T(8,128)(2,1)S(1)} %slice.6), channel_id=1, source_target_pairs={{0,24},{24,0},{8,16},{16,8},{1,25},{25,1},{9,17},{17,9},{2,26},{26... | collective-permute-start | bytes 589832 | tf_op jit(solution)/shard_map/ppermute | solution.py:96
  50.8 5.1 %collective-permute-start.4 = (bf16[4,128,512]{2,1,0:T(8,128)(2,1)S(1)}, bf16[4,128,512]{2,1,0:T(8,128)(2,1)S(1)}, u32[]{:S(2)}, u32[]{:S(2)}) collective-permute-start(bf16[4,128,512]{2,1,0:T(8,128)(2,1)S(1)} %bitcast.10), channel_id=1, source_target_pairs={{0,1},{1,0},{2,3},{3,2},{4,5},{5,4},{6,7},{7,6},{8,9},{9,8},{10,11... | collective-permute-start | bytes 1572872 | tf_op jit(solution)/shard_map/ppermute | solution.py:101
  56.9 45.1 %copy-start.3 = (f32[32,512]{1,0:T(8,128)S(1)}, f32[32,512]{1,0:T(8,128)}, u32[]{:S(2)}) copy-start(f32[32,512]{1,0:T(8,128)} %param.9) | copy-start | bytes 196612
  56.9 45.1 %copy-start.4 = (f32[32,512]{1,0:T(8,128)S(1)}, f32[32,512]{1,0:T(8,128)}, u32[]{:S(2)}) copy-start(f32[32,512]{1,0:T(8,128)} %param.8) | copy-start | bytes 196612

commit v4 on v3

--- a/solution.py
+++ b/solution.py
@@ -6,8 +6,9 @@
 from jax.sharding import Mesh, PartitionSpec as P
 
 STEP = 10
-AXES = ("z", "h", "x", "y", "c")
-SIZES = (12, 2, 4, 4, 2)
+AXES = ("zh", "zl", "h", "x", "y", "c")
+SIZES = (4, 3, 2, 4, 4, 2)
+GROUP = 3
 SWAP = ((0, 1), (1, 0))
 NEAR = ((0, 1), (1, 0), (2, 3), (3, 2))
 FAR = ((0, 3), (3, 0), (1, 2), (2, 1))
@@ -19,11 +20,15 @@
 
 
 def turn(grad_ref, keep_ref, near_ref, far_ref, turned):
-    me = lax.axis_index("x")
+    me, mine = lax.axis_index("x"), lax.axis_index("zl")
+    part = turned.shape[1] // GROUP
     for block in range(grad_ref.shape[1] // 128):
         flipped = grad_ref[:, block * 128 : (block + 1) * 128].T
+        slot = lax.rem(block // 2 % GROUP + GROUP - mine, GROUP)
+        row = slot * part + (block // (2 * GROUP) * 2 + block % 2) * 32
+        at = pl.ds(pl.multiple_of(row, 32), 32)
         for x in range(RING):
-            turned[x, block * 32 : (block + 1) * 32, :] = flipped[x * 32 : (x + 1) * 32]
+            turned[x, at, :] = flipped[x * 32 : (x + 1) * 32]
     width = keep_ref.shape[0]
     keep_ref[...] = turned[me]
     near_ref[:width] = turned[near(me)]
@@ -33,7 +38,7 @@
     far_ref[width:] = turned[across, width // 2 :, :]
 
 
-def project(keep_ref, near_ref, far_ref, left_ref, right_ref, mine_ref, other_ref, out_ref):
+def project(keep_ref, near_ref, far_ref, left_ref, right_ref, mine_ref, other_ref, own_ref, *sends):
     me = lax.axis_index("x")
     first = lax.axis_index("c") == 0
     width = keep_ref.shape[0]
@@ -52,7 +57,10 @@
         reduced = jnp.concatenate([low, high], axis=0)
         term = jnp.dot(grad, reduced, preferred_element_type=jnp.float32)
         total = term if total is None else total + term
-    out_ref[...] = total.astype(out_ref.dtype)
+    part = own_ref.shape[0]
+    own_ref[...] = total[:part]
+    for k, send_ref in enumerate(sends, 1):
+        send_ref[...] = total[k * part : (k + 1) * part].astype(send_ref.dtype)
 
 
 def share(partial_ref, copies_ref):
@@ -100,10 +108,16 @@
     mine, left, right = lax.optimization_barrier((mine, left, right))
     other = lax.ppermute(mine, "c", SWAP)
 
-    part = whole(project, 7, shape((width, rank), bf16), flops=2 * width * 4 * tokens * rank)(
-        keep, from_near, from_far, left, right, mine, other
-    )
-    part = lax.all_to_all(part, ("z", "h"), 0, 0, tiled=True).reshape(24, rows, rank)
+    part = width // GROUP
+    own, *sends = whole(
+        project,
+        7,
+        [shape((part, rank), f32)] + [shape((part, rank), bf16)] * (GROUP - 1),
+        flops=2 * width * 4 * tokens * rank,
+    )(keep, from_near, from_far, left, right, mine, other)
+    for k, send in enumerate(sends, 1):
+        own = own + lax.ppermute(send, "zl", [(z, (z + k) % GROUP) for z in range(GROUP)]).astype(f32)
+    part = lax.all_to_all(own.astype(bf16), ("zh", "h"), 0, 0, tiled=True).reshape(24 // GROUP, rows, rank)
     projected = jnp.sum(part.astype(f32), axis=0)
 
     new_first = 0.9 * first_moment + 0.1 * projected
@@ -120,7 +134,7 @@
 
 def solution(mesh):
     fine = Mesh(mesh.devices.reshape(SIZES), AXES)
-    dp, fsdp = ("z", "h", "x"), ("y", "c")
+    dp, fsdp = ("zh", "zl", "h", "x"), ("y", "c")
     in_specs = (P(dp, fsdp), P(dp, fsdp), P(fsdp, None), P(fsdp + dp, None), P(fsdp + dp, None))
     out_specs = (P(fsdp + dp, None), P(fsdp + dp, None), P(None, dp, fsdp))
     return jax.shard_map(shards, mesh=fine, in_specs=in_specs, out_specs=out_specs, check_vma=False)

time: 119 us -> 118 us (level)
  blocking collectives: 77.1 us -> 59.6 us
  waiting for transfers between devices: 10.2 us -> 20.7 us
  starting transfers between devices: 23.5 us -> 29.8 us
    all_to_all x1, blocking collectives: 44.9 us -> 30.3 us  [shards(): lax.all_to_all(own.astype(bf16), ('zh', 'h'), 0, 0, tiled=True)]
    ppermute x0 -> x2, waiting for transfers between devices: none -> 10.5 us  [shards(): lax.ppermute(send, 'zl', [(z, (z + k) % GROUP) for z in range(GROUP)])]
    ppermute x0 -> x2, starting transfers between devices: none -> 6.31 us  [shards(): lax.ppermute(send, 'zl', [(z, (z + k) % GROUP) for z in range(GROUP)])]
    all_gather x1, blocking collectives: 6.86 us -> 3.98 us  [shards(): lax.all_gather(grouped, 'c', axis=1, tiled=False).reshape(8 * rows, rank)]
  transfers between devices with their start and end apart: 6 -> 8, of which waited for: 4 -> 6; matrix products, arithmetic and copies ran while one was open for 0% -> 0% of each run, Pallas kernels for 0% -> 0%
where the time goes in v4:
time: 118 us; the launch traced here: 117 us
  blocking collectives  59.6 us (51%)
  starting transfers between devices  29.8 us (25%)
  waiting for transfers between devices  20.7 us (18%)
  Pallas kernels  2.4 us (2%)
  matrix products  1.69 us (1%)
  local copies, waits for them, and re-layouts  1.55 us (1%)
    all_to_all x1, blocking collectives, shards(): lax.all_to_all(own.astype(bf16), ('zh', 'h'), 0, 0, tiled=True)  30.3 us
    all_to_all x1, blocking collectives, shards(): lax.all_to_all(partial, ('c', 'y'), 0, 0, tiled=True)  18.1 us
    ppermute x2, waiting for transfers between devices, shards(): lax.ppermute(send, 'zl', [(z, (z + k) % GROUP) for z in range(GROUP)])  10.5 us
    all_to_all x1, blocking collectives, shards(): lax.all_to_all(copies, 'y', 0, 0, tiled=True).reshape(4, rows, rank)  7.2 us
    ppermute x2, starting transfers between devices, shards(): lax.ppermute(send, 'zl', [(z, (z + k) % GROUP) for z in range(GROUP)])  6.31 us
    ppermute x1, waiting for transfers between devices, shards(): right = lax.ppermute(from_far[width:], 'x', NEAR)  5.56 us
    all_to_all x1, starting transfers between devices, shards(): lax.all_to_all(copies, ('x', 'y'), 0, 0, tiled=True)  5.22 us
    all_gather x1, blocking collectives, shards(): lax.all_gather(grouped, 'c', axis=1, tiled=False).reshape(8 * rows, rank)  3.98 us
  transfers between devices with their start and end apart: 8, of which 6 were waited for; matrix products, arithmetic and copies ran while one was open for 0% of the time, Pallas kernels for 0%

profile of v4, /device:TPU:1, one launch (start us, length us, event | category | flops | bytes accessed | tf_op | source)
XLA Modules:
  0.0 117.4 jit_solution(8852880834454605467)
XLA Ops:
  0.6 0.0 copy-start
  0.6 0.0 copy-start.1
  0.7 1.5 %copy-done.1 = bf16[256,3072]{1,0:T(8,128)(2,1)S(1)} copy-done((bf16[256,3072]{1,0:T(8,128)(2,1)S(1)}, bf16[256,3072]{1,0:T(8,128)(2,1)}, u32[]{:S(2)}) %copy-start.1) | copy-done | bytes 1572888
  2.1 0.6 shard_map.76
  2.7 3.9 %collective-permute-start = (bf16[1152,256]{1,0:T(8,128)(2,1)S(1)}, bf16[1152,256]{1,0:T(8,128)(2,1)S(1)}, u32[]{:S(2)}, u32[]{:S(2)}) collective-permute-start(bf16[1152,256]{1,0:T(8,128)(2,1)S(1)} %get-tuple-element.16), channel_id=1, source_target_pairs={{0,8},{8,0},{16,24},{24,16},{1,9},{9,1},{17,25},{25,17},{2,10},{10... | collective-permute-start | bytes 1769480 | tf_op jit(solution)/shard_map/ppermute | solution.py:97
  6.7 3.7 %collective-permute-start.1 = (bf16[1152,256]{1,0:T(8,128)(2,1)S(1)}, bf16[1152,256]{1,0:T(8,128)(2,1)S(1)}, u32[]{:S(2)}, u32[]{:S(2)}) collective-permute-start(bf16[1152,256]{1,0:T(8,128)(2,1)S(1)} %get-tuple-element.17), channel_id=1, source_target_pairs={{0,24},{24,0},{8,16},{16,8},{1,25},{25,1},{9,17},{17,9},{2,26},{26... | collective-permute-start | bytes 1769480 | tf_op jit(solution)/shard_map/ppermute | solution.py:98
  10.4 0.4 convolution_convert_fusion.1
  10.9 18.1 %all_to_all.30.partial_ref = bf16[8,32,512]{2,1,0:T(8,128)(2,1)S(1)} all-to-all(bf16[8,32,512]{2,1,0:T(8,128)(2,1)S(1)} %bitcast.13), channel_id=1, replica_groups=mesh['zh'=4,'zl'=3,'h'=2,'x'=4,'y'=4,'c'=2] {'c','y'}, dimensions={0} | all-to-all | bytes 524288 | tf_op jit(solution)/shard_map/all_to_all | solution.py:101
  29.0 0.0 collective-permute-done.near_ref
  29.0 0.0 collective-permute-done.1.far_ref
  29.0 0.9 shard_map.77
  29.9 5.2 %all-to-all-start.1 = ((bf16[16,32,512]{2,1,0:T(8,128)(2,1)}), bf16[16,32,512]{2,1,0:T(8,128)(2,1)S(1)}, u32[]{:S(2)}, u32[]{:S(2)}) async-start(bf16[16,32,512]{2,1,0:T(8,128)(2,1)} %shard_map.77), calls=%async_computation.1 | async-start | bytes 1048576 | tf_op jit(solution)/shard_map/all_to_all | solution.py:107
  35.1 3.3 %collective-permute-start.3 = (bf16[384,256]{1,0:T(8,128)(2,1)S(1)}, bf16[384,256]{1,0:T(8,128)(2,1)S(1)}, u32[]{:S(2)}, u32[]{:S(2)}) collective-permute-start(bf16[384,256]{1,0:T(8,128)(2,1)S(1)} %slice.7), channel_id=1, source_target_pairs={{0,8},{8,0},{16,24},{24,16},{1,9},{9,1},{17,25},{25,17},{2,10},{10... | collective-permute-start | bytes 589832 | tf_op jit(solution)/shard_map/ppermute | solution.py:105
  38.4 3.7 %collective-permute-start.2 = (bf16[384,256]{1,0:T(8,128)(2,1)S(1)}, bf16[384,256]{1,0:T(8,128)(2,1)S(1)}, u32[]{:S(2)}, u32[]{:S(2)}) collective-permute-start(bf16[384,256]{1,0:T(8,128)(2,1)S(1)} %slice.6), channel_id=1, source_target_pairs={{0,24},{24,0},{8,16},{16,8},{1,25},{25,1},{9,17},{17,9},{2,26},{26... | collective-permute-start | bytes 589832 | tf_op jit(solution)/shard_map/ppermute | solution.py:104
  42.1 5.6 %collective-permute-done.3.right_ref = bf16[384,256]{1,0:T(8,128)(2,1)S(1)} collective-permute-done((bf16[384,256]{1,0:T(8,128)(2,1)S(1)}, bf16[384,256]{1,0:T(8,128)(2,1)S(1)}, u32[]{:S(2)}, u32[]{:S(2)}) %collective-permute-start.3) | collective-permute-done | bytes 196640 | tf_op jit(solution)/shard_map/ppermute | solution.py:105
  47.7 1.2 %collective-permute-done.2.left_ref = bf16[384,256]{1,0:T(8,128)(2,1)S(1)} collective-permute-done((bf16[384,256]{1,0:T(8,128)(2,1)S(1)}, bf16[384,256]{1,0:T(8,128)(2,1)S(1)}, u32[]{:S(2)}, u32[]{:S(2)}) %collective-permute-start.2) | collective-permute-done | bytes 196640 | tf_op jit(solution)/shard_map/ppermute | solution.py:104
  48.9 1.9 %all-to-all-done.1 = bf16[16,32,512]{2,1,0:T(8,128)(2,1)S(1)} async-done(((bf16[16,32,512]{2,1,0:T(8,128)(2,1)}), bf16[16,32,512]{2,1,0:T(8,128)(2,1)S(1)}, u32[]{:S(2)}, u32[]{:S(2)}) %all-to-all-start.1) | async-done | bytes 524320 | tf_op jit(solution)/shard_map/all_to_all | solution.py:107
  50.8 3.6 %collective-permute-start.4 = (bf16[4,128,512]{2,1,0:T(8,128)(2,1)S(1)}, bf16[4,128,512]{2,1,0:T(8,128)(2,1)S(1)}, u32[]{:S(2)}, u32[]{:S(2)}) collective-permute-start(bf16[4,128,512]{2,1,0:T(8,128)(2,1)S(1)} %bitcast.9), channel_id=1, source_target_pairs={{0,1},{1,0},{2,3},{3,2},{4,5},{5,4},{6,7},{7,6},{8,9},{9,8},{10,11... | collective-permute-start | bytes 1572872 | tf_op jit(solution)/shard_map/ppermute | solution.py:109
  54.5 1.5 %collective-permute-done.4.other_ref = bf16[4,128,512]{2,1,0:T(8,128)(2,1)S(1)} collective-permute-done((bf16[4,128,512]{2,1,0:T(8,128)(2,1)S(1)}, bf16[4,128,512]{2,1,0:T(8,128)(2,1)S(1)}, u32[]{:S(2)}, u32[]{:S(2)}) %collective-permute-start.4) | collective-permute-done | bytes 524320 | tf_op jit(solution)/shard_map/ppermute | solution.py:109
  56.0 1.0 shard_map.78
  57.0 0.0 copy-start.3
  57.0 0.0 copy-start.4
  57.0 2.1 %collective-permute-start.5 = (bf16[256,512]{1,0:T(8,128)(2,1)S(1)}, bf16[256,512]{1,0:T(8,128)(2,1)S(1)}, u32[]{:S(2)}, u32[]{:S(2)}) collective-permute-start(bf16[256,512]{1,0:T(8,128)(2,1)S(1)} %get-tuple-element.25), channel_id=1, source_target_pairs={{0,64},{64,128},{128,0},{1,65},{65,129},{129,1},{2,66},{66,130},{1... | collective-permute-start | bytes 786440 | tf_op jit(solution)/shard_map/ppermute | solution.py:119
  59.0 4.3 %collective-permute-start.6 = (bf16[256,512]{1,0:T(8,128)(2,1)S(1)}, bf16[256,512]{1,0:T(8,128)(2,1)S(1)}, u32[]{:S(2)}, u32[]{:S(2)}) collective-permute-start(bf16[256,512]{1,0:T(8,128)(2,1)S(1)} %get-tuple-element.26), channel_id=1, source_target_pairs={{0,128},{64,0},{128,64},{1,129},{65,1},{129,65},{2,130},{66,2},{13... | collective-permute-start | bytes 786440 | tf_op jit(solution)/shard_map/ppermute | solution.py:119
  63.3 4.2 %collective-permute-done.5 = bf16[256,512]{1,0:T(8,128)(2,1)S(1)} collective-permute-done((bf16[256,512]{1,0:T(8,128)(2,1)S(1)}, bf16[256,512]{1,0:T(8,128)(2,1)S(1)}, u32[]{:S(2)}, u32[]{:S(2)}) %collective-permute-start.5) | collective-permute-done | bytes 262176 | tf_op jit(solution)/shard_map/ppermute | solution.py:119
  67.5 6.3 %collective-permute-done.6 = bf16[256,512]{1,0:T(8,128)(2,1)S(1)} collective-permute-done((bf16[256,512]{1,0:T(8,128)(2,1)S(1)}, bf16[256,512]{1,0:T(8,128)(2,1)S(1)}, u32[]{:S(2)}, u32[]{:S(2)}) %collective-permute-start.6) | collective-permute-done | bytes 262176 | tf_op jit(solution)/shard_map/ppermute | solution.py:119
  73.8 0.1 add_convert_fusion
  73.9 30.3 %all_to_all.31 = bf16[8,32,512]{2,1,0:T(8,128)(2,1)S(1)} all-to-all(bf16[8,32,512]{2,1,0:T(8,128)(2,1)S(1)} %bitcast.11), channel_id=1, replica_groups=mesh['zh'=4,'zl'=3,'h'=2,'x'=4,'y'=4,'c'=2] {'zh','h'}, dimensions={0} | all-to-all | bytes 524288 | tf_op jit(solution)/shard_map/all_to_all | solution.py:120
  104.3 0.7 divide_convert_fusion
  105.0 7.2 %all_to_all.32 = bf16[4,32,512]{2,1,0:T(8,128)(2,1)S(1)} all-to-all(bf16[4,32,512]{2,1,0:T(8,128)(2,1)S(1)} %broadcast_in_dim.2), channel_id=1, replica_groups=mesh['zh'=4,'zl'=3,'h'=2,'x'=4,'y'=4,'c'=2] {'y'}, dimensions={0} | all-to-all | bytes 262144 | tf_op jit(solution)/shard_map/all_to_all | solution.py:129
  112.2 4.0 %all-gather = bf16[4,64,512]{2,1,0:T(8,128)(2,1)S(1)} all-gather(bf16[4,32,512]{2,1,0:T(8,128)(2,1)S(1)} %all_to_all.32), channel_id=2, replica_groups=mesh['zh'=4,'zl'=3,'h'=2,'x'=4,'y'=4,'c'=2] {'c'}, dimensions={1}, use_global_device_ids=true | all-gather | bytes 393216 | tf_op jit(solution)/shard_map/all_gather | solution.py:130
  116.1 1.3 %convolution_convert_fusion = bf16[256,1024]{1,0:T(8,128)(2,1)} fusion(bf16[256,512]{1,0:T(8,128)(2,1)S(1)} %bitcast.12, bf16[1024,512]{1,0:T(8,128)(2,1)S(1)} %copy-done), kind=kOutput, calls=%fused_computation | convolution fusion | flops 268697600 | bytes 1835008 | tf_op jit(solution)/shard_map/dot_general | solution.py:131
  (9 shorter events, 0.1 us)
Async XLA Ops:
  0.6 9.8 %copy-start = (bf16[1024,512]{1,0:T(8,128)(2,1)S(1)}, bf16[1024,512]{1,0:T(8,128)(2,1)}, u32[]{:S(2)}) copy-start(bf16[1024,512]{1,0:T(8,128)(2,1)} %param.7) | copy-start | bytes 3145732
  0.6 1.5 %copy-start.1 = (bf16[256,3072]{1,0:T(8,128)(2,1)S(1)}, bf16[256,3072]{1,0:T(8,128)(2,1)}, u32[]{:S(2)}) copy-start(bf16[256,3072]{1,0:T(8,128)(2,1)} %grad_ref.1) | copy-start | bytes 4718596
  2.1 8.3 %copy-start.2 = (bf16[256,1024]{1,0:T(8,128)(2,1)S(1)}, bf16[256,1024]{1,0:T(8,128)(2,1)}, u32[]{:S(2)}) copy-start(bf16[256,1024]{1,0:T(8,128)(2,1)} %param.5) | copy-start | bytes 1572868
  2.7 26.3 %collective-permute-start = (bf16[1152,256]{1,0:T(8,128)(2,1)S(1)}, bf16[1152,256]{1,0:T(8,128)(2,1)S(1)}, u32[]{:S(2)}, u32[]{:S(2)}) collective-permute-start(bf16[1152,256]{1,0:T(8,128)(2,1)S(1)} %get-tuple-element.16), channel_id=1, source_target_pairs={{0,8},{8,0},{16,24},{24,16},{1,9},{9,1},{17,25},{25,17},{2,10},{10... | collective-permute-start | bytes 1769480 | tf_op jit(solution)/shard_map/ppermute | solution.py:97
  6.7 22.3 %collective-permute-start.1 = (bf16[1152,256]{1,0:T(8,128)(2,1)S(1)}, bf16[1152,256]{1,0:T(8,128)(2,1)S(1)}, u32[]{:S(2)}, u32[]{:S(2)}) collective-permute-start(bf16[1152,256]{1,0:T(8,128)(2,1)S(1)} %get-tuple-element.17), channel_id=1, source_target_pairs={{0,24},{24,0},{8,16},{16,8},{1,25},{25,1},{9,17},{17,9},{2,26},{26... | collective-permute-start | bytes 1769480 | tf_op jit(solution)/shard_map/ppermute | solution.py:98
  29.9 21.0 %all-to-all-start.1 = ((bf16[16,32,512]{2,1,0:T(8,128)(2,1)}), bf16[16,32,512]{2,1,0:T(8,128)(2,1)S(1)}, u32[]{:S(2)}, u32[]{:S(2)}) async-start(bf16[16,32,512]{2,1,0:T(8,128)(2,1)} %shard_map.77), calls=%async_computation.1 | async-start | bytes 1048576 | tf_op jit(solution)/shard_map/all_to_all | solution.py:107
  35.1 12.5 %collective-permute-start.3 = (bf16[384,256]{1,0:T(8,128)(2,1)S(1)}, bf16[384,256]{1,0:T(8,128)(2,1)S(1)}, u32[]{:S(2)}, u32[]{:S(2)}) collective-permute-start(bf16[384,256]{1,0:T(8,128)(2,1)S(1)} %slice.7), channel_id=1, source_target_pairs={{0,8},{8,0},{16,24},{24,16},{1,9},{9,1},{17,25},{25,17},{2,10},{10... | collective-permute-start | bytes 589832 | tf_op jit(solution)/shard_map/ppermute | solution.py:105
  38.4 10.5 %collective-permute-start.2 = (bf16[384,256]{1,0:T(8,128)(2,1)S(1)}, bf16[384,256]{1,0:T(8,128)(2,1)S(1)}, u32[]{:S(2)}, u32[]{:S(2)}) collective-permute-start(bf16[384,256]{1,0:T(8,128)(2,1)S(1)} %slice.6), channel_id=1, source_target_pairs={{0,24},{24,0},{8,16},{16,8},{1,25},{25,1},{9,17},{17,9},{2,26},{26... | collective-permute-start | bytes 589832 | tf_op jit(solution)/shard_map/ppermute | solution.py:104
  50.8 5.1 %collective-permute-start.4 = (bf16[4,128,512]{2,1,0:T(8,128)(2,1)S(1)}, bf16[4,128,512]{2,1,0:T(8,128)(2,1)S(1)}, u32[]{:S(2)}, u32[]{:S(2)}) collective-permute-start(bf16[4,128,512]{2,1,0:T(8,128)(2,1)S(1)} %bitcast.9), channel_id=1, source_target_pairs={{0,1},{1,0},{2,3},{3,2},{4,5},{5,4},{6,7},{7,6},{8,9},{9,8},{10,11... | collective-permute-start | bytes 1572872 | tf_op jit(solution)/shard_map/ppermute | solution.py:109
  57.0 47.3 %copy-start.3 = (f32[32,512]{1,0:T(8,128)S(1)}, f32[32,512]{1,0:T(8,128)}, u32[]{:S(2)}) copy-start(f32[32,512]{1,0:T(8,128)} %param.9) | copy-start | bytes 196612
  57.0 47.3 %copy-start.4 = (f32[32,512]{1,0:T(8,128)S(1)}, f32[32,512]{1,0:T(8,128)}, u32[]{:S(2)}) copy-start(f32[32,512]{1,0:T(8,128)} %param.8) | copy-start | bytes 196612
  57.0 10.5 %collective-permute-start.5 = (bf16[256,512]{1,0:T(8,128)(2,1)S(1)}, bf16[256,512]{1,0:T(8,128)(2,1)S(1)}, u32[]{:S(2)}, u32[]{:S(2)}) collective-permute-start(bf16[256,512]{1,0:T(8,128)(2,1)S(1)} %get-tuple-element.25), channel_id=1, source_target_pairs={{0,64},{64,128},{128,0},{1,65},{65,129},{129,1},{2,66},{66,130},{1... | collective-permute-start | bytes 786440 | tf_op jit(solution)/shard_map/ppermute | solution.py:119
  59.0 14.7 %collective-permute-start.6 = (bf16[256,512]{1,0:T(8,128)(2,1)S(1)}, bf16[256,512]{1,0:T(8,128)(2,1)S(1)}, u32[]{:S(2)}, u32[]{:S(2)}) collective-permute-start(bf16[256,512]{1,0:T(8,128)(2,1)S(1)} %get-tuple-element.26), channel_id=1, source_target_pairs={{0,128},{64,0},{128,64},{1,129},{65,1},{129,65},{2,130},{66,2},{13... | collective-permute-start | bytes 786440 | tf_op jit(solution)/shard_map/ppermute | solution.py:119
